TPU v7x, 32 devices: a whole 2x2x4 slice. The times are simulated.
32 devices in a mesh: section: 2 (over x), expert: 16 (over z, y, core).
Axes of the slice: x: 2, y: 2, z: 4, core: 2. Of those that a mesh axis runs over, the one named last changes fastest.
Arguments:
- inputs: bfloat16 [2, 128, 2048], P(None, 'expert'), may hold values from -6 to 6
- route_ids: int32 [2, 2, 128, 8], P('section', None, 'expert'), may hold values from 0 to 15, all different within a row; in each aligned block of 8 rows (0 to 7, 8 to 15, ..., all dimensions but the last counted through in order) at most 8 rows name the same one
- route_gates: float32 [2, 2, 128, 8], P('section', None, 'expert'), may hold values from 0.1 to 1
- w_gate: bfloat16 [2, 16, 2048, 768], P('section', 'expert'), may hold values from -0.125 to 0.125
- w_up: bfloat16 [2, 16, 2048, 768], P('section', 'expert'), may hold values from -0.125 to 0.125
- w_down: bfloat16 [2, 16, 768, 2048], P('section', 'expert'), may hold values from -0.21875 to 0.21875
- cotangent: bfloat16 [2, 128, 2048], P(None, 'expert'), may hold values from -6 to 6
Outputs:
- section_out: bfloat16 [2, 2, 128, 2048], P('section', None, 'expert')
- grad_input: bfloat16 [2, 2, 128, 2048], P('section', None, 'expert')
- grad_gates: float32 [2, 2, 128, 8], P('section', None, 'expert')
- grad_w_gate: bfloat16 [2, 16, 2048, 768], P('section', 'expert')
- grad_w_up: bfloat16 [2, 16, 2048, 768], P('section', 'expert')
- grad_w_down: bfloat16 [2, 16, 768, 2048], P('section', 'expert')
Inputs may be any that keep to these rules, and one draw needn't show every extreme that they name: `route_ids`: A token's 8 ids differ. In each layer and micro-batch, the 8 tokens of one device name no expert more than 8 times, a bound that some block reaches; every expert is named somewhere.
All inputs are finite; a program needn't handle non-finite values.
Results may differ from a plain program's by a relative error of at most 0.023.
Values may be sent and summed in bfloat16 or wider, within the bound.
A program may use at most 128 MiB of HBM per device.

v0:
```python
import functools

import jax
import jax.numpy as jnp
from jax import lax
from jax.experimental import pallas as pl
from jax.experimental.pallas import tpu as pltpu
from jax.sharding import PartitionSpec as P

EPS = 1e-06
F32 = jnp.float32
BF16 = jnp.bfloat16
LANES = 128
TILE = 256


def nt_dot(a, b):
    return lax.dot_general(a, b, (((1,), (1,)), ((), ())), preferred_element_type=F32)


def bit_orders(n):
    bits = n.bit_length() - 1
    high_first = list(range(bits - 1, -1, -1))
    across = [1] + [b for b in high_first if b not in (0, 1)] + [0]
    return high_first, across


def kernel(
    sections, n, x_ref, ids_ref, gts_ref, cot_ref, wg_hbm, wu_hbm, wd_hbm,
    so_ref, gi_ref, gg_ref, nx_hbm, hg_hbm, ag_hbm, ggp_hbm, gup_hbm,
    wg, wu, wd, xin, gin, nown, xst, gst, agx, agg, tg, tt, ttr,
    gc, gp, up, hid, hg, ggp, gup, acc, sb, rb, sb0, rb0,
    ag_s, ag_r, rs_s, rs_r, rl_s, rl_r, loc,
):
    mb, tok, width = x_ref.shape
    top = ids_ref.shape[2]
    ff = wg.shape[1]
    steps = n.bit_length() - 1
    rows1 = n * tok
    rows = mb * rows1
    me = lax.axis_index("expert")
    sec = lax.axis_index("section")
    last = sections - 1
    orders = [bit_orders(n)[m % 2] for m in range(mb)]

    def bit_of(b):
        return (me // (1 << b)) % 2

    def peer(b):
        return me + (1 << b) * (1 - 2 * bit_of(b))

    place = [sum(bit_of(b) * (1 << k) for k, b in enumerate(order)) for order in orders]

    def other(m, k):
        r = place[m]
        return r + (1 << k) * (1 - 2 * ((r // (1 << k)) % 2))

    def base_of(r, k):
        return (r // (1 << k)) * (1 << k)

    def remote(src, dst, ssem, rsem, b):
        return pltpu.make_async_remote_copy(
            src_ref=src, dst_ref=dst, send_sem=ssem, recv_sem=rsem,
            device_id={"expert": peer(b)}, device_id_type=pl.DeviceIdType.MESH,
        )

    weights = [
        pltpu.make_async_copy(a, b, loc.at[i])
        for i, (a, b) in enumerate(((wg_hbm, wg), (wu_hbm, wu), (wd_hbm, wd)))
    ]
    for c in weights:
        c.start()

    barrier = pltpu.get_barrier_semaphore()
    for b in range(steps):
        pl.semaphore_signal(
            barrier, inc=1, device_id={"expert": peer(b)}, device_id_type=pl.DeviceIdType.MESH
        )

    def hello(ok, step):
        @pl.when(ok)
        def _():
            pl.semaphore_signal(
                barrier, inc=1, device_id={"section": sec + step},
                device_id_type=pl.DeviceIdType.MESH,
            )

    hello(sec > 0, -1)
    hello(sec < last, 1)

    lane = lax.broadcasted_iota(jnp.int32, (tok, LANES), 1)
    for m in range(mb):
        dense = jnp.zeros((tok, LANES), F32)
        for k in range(top):
            dense = dense + jnp.where(
                lane == ids_ref[m, :, k : k + 1], gts_ref[m, :, k : k + 1], 0.0
            )
        tg[m, place[m]] = dense

    beside = (sec > 0).astype(jnp.int32) + (sec < last).astype(jnp.int32)
    pl.semaphore_wait(barrier, steps + beside)

    def small_copy(m, k):
        part = tg.at[m, pl.ds(base_of(place[m], k), 1 << k)]
        return remote(part, part, ag_s.at[0, m, k], ag_r.at[0, m, k], orders[m][k])

    def row_copy(which, own, staged, full, m, k):
        sems = ag_s.at[which, m, k], ag_r.at[which, m, k]
        if k == 0:
            return remote(own.at[m], staged.at[m], *sems, orders[m][0])
        part = full.at[m, pl.ds(base_of(place[m], k) // 2, 1 << (k - 1))]
        return remote(part, part, *sems, orders[m][k])

    def gather_rows(which, own, staged, full):
        for k in range(steps):
            copies = [row_copy(which, own, staged, full, m, k) for m in range(mb)]
            for c in copies:
                c.start()
            for m, c in enumerate(copies):
                c.wait()
                if k == 0:
                    mine = own[m].astype(F32)
                    theirs = staged[m].astype(F32)
                    low = place[m] % 2 == 0
                    pair = jnp.concatenate(
                        [jnp.where(low, mine, theirs), jnp.where(low, theirs, mine)], axis=0
                    )
                    full[m, place[m] // 2] = pair.astype(BF16)

    def table_copy(m, k):
        theirs = base_of(other(m, k), k)
        return remote(
            tt.at[m, pl.ds(theirs, 1 << k)], ttr.at[m, pl.ds(1 << k, 1 << k)],
            rs_s.at[2, m, k], rs_r.at[2, m, k], orders[m][k],
        )

    def reduce_rows(which, table):
        def when_table(act):
            if table is True:
                act()
            elif table is not None:
                pl.when(table)(act)

        def row_part(m, k):
            sems = rs_s.at[which, m, k], rs_r.at[which, m, k]
            theirs = base_of(other(m, k), k)
            if k == 0:
                sb0[which, m] = acc[m, theirs].astype(BF16)
                return remote(sb0.at[which, m], rb0.at[which, m], *sems, orders[m][0])
            half = 1 << (k - 1)

            def pack(i, carry):
                pair = acc[m, pl.ds(theirs + 2 * i, 2)].reshape(2 * tok, width)
                sb[which, m, theirs // 2 + i] = pair.astype(BF16)
                return carry

            lax.fori_loop(0, half, pack, 0)
            return remote(
                sb.at[which, m, pl.ds(theirs // 2, half)], rb.at[which, m, pl.ds(half, half)],
                *sems, orders[m][k],
            )

        for k in reversed(range(steps)):
            copies = []
            for m in range(mb):
                copies.append(row_part(m, k))
                copies[m].start()

            def start_tables():
                for m in range(mb):
                    table_copy(m, k).start()

            when_table(start_tables)
            for m in range(mb):
                copies[m].wait()
                mine = base_of(place[m], k)
                if k == 0:
                    acc[m, mine] = acc[m, mine] + rb0[which, m].astype(F32)
                else:
                    half = 1 << (k - 1)

                    def add(i, carry):
                        got = rb[which, m, half + i].astype(F32).reshape(2, tok, width)
                        spot = pl.ds(mine + 2 * i, 2)
                        acc[m, spot] = acc[m, spot] + got
                        return carry

                    lax.fori_loop(0, half, add, 0)

            def finish_tables():
                for m in range(mb):
                    table_copy(m, k).wait()
                    mine = pl.ds(base_of(place[m], k), 1 << k)
                    tt[m, mine] = tt[m, mine] + ttr[m, pl.ds(1 << k, 1 << k)]

            when_table(finish_tables)

    @pl.when(sec == last)
    def _():
        gin[...] = cot_ref[...]
        gather_rows(2, gin, gst, agg)

    for k in range(steps):
        copies = [small_copy(m, k) for m in range(mb)]
        for c in copies:
            c.start()
        for c in copies:
            c.wait()
    all_lanes = lax.broadcasted_iota(jnp.int32, (rows, LANES), 1)
    gc[...] = jnp.sum(
        jnp.where(all_lanes == me, tg[...].reshape(rows, LANES), 0.0), axis=1, keepdims=True
    )

    def relay(which, src, dst, step):
        return pltpu.make_async_remote_copy(
            src_ref=src, dst_ref=dst, send_sem=rl_s.at[which], recv_sem=rl_r.at[which],
            device_id={"section": sec + step}, device_id_type=pl.DeviceIdType.MESH,
        )

    @pl.when(sec == 0)
    def _():
        xin[...] = x_ref[...]

    @pl.when(sec > 0)
    def _():
        relay(0, so_ref, xin, 0).wait_recv()

    x_float = xin[...].astype(F32)
    scale = lax.rsqrt(jnp.mean(x_float * x_float, axis=-1, keepdims=True) + EPS)
    nown[...] = (x_float * scale).astype(BF16)
    gather_rows(1, nown, xst, agx)
    keep = [pltpu.make_async_copy(agx, nx_hbm, loc.at[3])]
    keep[0].start()
    for c in weights:
        c.wait()

    def hidden_tile(j, carry):
        at = pl.ds(pl.multiple_of(j * TILE, TILE), TILE)
        data = agx[...].reshape(rows, width)
        gate = jnp.dot(data, wg[:, at], preferred_element_type=F32)
        upper = jnp.dot(data, wu[:, at], preferred_element_type=F32)
        gp[:, at] = gate
        up[:, at] = upper
        hid[:, at] = (gate * jax.nn.sigmoid(gate) * upper).astype(BF16)
        return carry

    lax.fori_loop(0, ff // TILE, hidden_tile, 0)

    def down_and_out(table):
        def down_tile(j, carry):
            at = pl.ds(pl.multiple_of(j * TILE, TILE), TILE)
            out = jnp.dot(hid[...], wd[:, at], preferred_element_type=F32) * gc[...]
            acc[:, :, :, at] = out.reshape(mb, n, tok, TILE)
            return carry

        lax.fori_loop(0, width // TILE, down_tile, 0)
        reduce_rows(0, table)
        for m in range(mb):
            so_ref[m] = (xin[m].astype(F32) + acc[m, place[m]]).astype(BF16)

    @pl.when(sec < last)
    def _():
        down_and_out(None)
        relay(0, so_ref, xin, 1).start()
        relay(1, gi_ref, gin, 0).wait_recv()
        gather_rows(2, gin, gst, agg)

    keep.append(pltpu.make_async_copy(agg, ag_hbm, loc.at[4]))
    keep[1].start()

    def back_tile(j, total):
        at = pl.ds(pl.multiple_of(j * TILE, TILE), TILE)
        raw = nt_dot(agg[...].reshape(rows, width), wd[at, :])
        gate, upper = gp[:, at], up[:, at]
        sigma = jax.nn.sigmoid(gate)
        active = gate * sigma
        total = total + jnp.sum(active * upper * raw, axis=1, keepdims=True)
        scaled = raw * gc[...]
        ggp[:, at] = (scaled * upper * sigma * (1.0 + gate * (1.0 - sigma))).astype(BF16)
        gup[:, at] = (scaled * active).astype(BF16)
        hg[:, at] = (active * upper * gc[...]).astype(BF16)
        return total

    total = lax.fori_loop(0, ff // TILE, back_tile, jnp.zeros((rows, 1), F32))
    tt[...] = jnp.where(all_lanes == me, total, 0.0).reshape(mb, n, tok, LANES)
    for i, (a, b) in enumerate(((hg, hg_hbm), (ggp, ggp_hbm), (gup, gup_hbm))):
        keep.append(pltpu.make_async_copy(a, b, loc.at[5 + i]))
        keep[-1].start()

    def norm_tile(j, carry):
        at = pl.ds(pl.multiple_of(j * TILE, TILE), TILE)
        out = nt_dot(ggp[...], wg[at, :]) + nt_dot(gup[...], wu[at, :])
        acc[:, :, :, at] = out.reshape(mb, n, tok, TILE)
        return carry

    lax.fori_loop(0, width // TILE, norm_tile, 0)
    reduce_rows(1, sec < last)
    for m in range(mb):
        xf = xin[m].astype(F32)
        sc = lax.rsqrt(jnp.mean(xf * xf, axis=-1, keepdims=True) + EPS)
        gn = acc[m, place[m]]
        inner = jnp.mean(gn * xf, axis=-1, keepdims=True)
        gi_ref[m] = (gin[m].astype(F32) + sc * gn - xf * (sc * sc * sc) * inner).astype(BF16)

    @pl.when(sec > 0)
    def _():
        relay(1, gi_ref, gin, -1).start()

    @pl.when(sec == last)
    def _():
        down_and_out(True)

    column = lax.broadcasted_iota(jnp.int32, (tok, top), 1)
    for m in range(mb):
        table = tt[m, place[m]]
        picked = jnp.zeros((tok, top), F32)
        for k in range(top):
            value = jnp.sum(
                jnp.where(lane == ids_ref[m, :, k : k + 1], table, 0.0), axis=1, keepdims=True
            )
            picked = picked + jnp.where(column == k, value, 0.0)
        gg_ref[m] = picked

    @pl.when(sec < last)
    def _():
        relay(0, so_ref, xin, 1).wait_send()

    @pl.when(sec > 0)
    def _():
        relay(1, gi_ref, gin, -1).wait_send()

    for c in keep:
        c.wait()


def body(sections, n, inputs, route_ids, route_gates, w_gate, w_up, w_down, cotangent):
    mb, tok, width = inputs.shape
    top = route_ids.shape[3]
    ff = w_gate.shape[3]
    rows = mb * n * tok
    steps = n.bit_length() - 1
    pairs = (mb, n // 2, 2 * tok, width)
    own = (mb, tok, width)
    vmem = pl.BlockSpec(memory_space=pltpu.VMEM)
    anywhere = pl.BlockSpec(memory_space=pl.ANY)
    sem = pltpu.SemaphoreType.DMA
    wide = pltpu.VMEM((rows, ff), BF16)
    table = pltpu.VMEM((mb, n, tok, LANES), F32)
    outs = pl.pallas_call(
        functools.partial(kernel, sections, n),
        out_shape=(
            jax.ShapeDtypeStruct(own, BF16),
            jax.ShapeDtypeStruct(own, BF16),
            jax.ShapeDtypeStruct((mb, tok, top), F32),
            jax.ShapeDtypeStruct(pairs, BF16),
            jax.ShapeDtypeStruct((rows, ff), BF16),
            jax.ShapeDtypeStruct(pairs, BF16),
            jax.ShapeDtypeStruct((rows, ff), BF16),
            jax.ShapeDtypeStruct((rows, ff), BF16),
        ),
        in_specs=[vmem] * 4 + [anywhere] * 3,
        out_specs=(vmem,) * 3 + (anywhere,) * 5,
        scratch_shapes=[
            pltpu.VMEM((width, ff), BF16),
            pltpu.VMEM((width, ff), BF16),
            pltpu.VMEM((ff, width), BF16),
            pltpu.VMEM(own, BF16),
            pltpu.VMEM(own, BF16),
            pltpu.VMEM(own, BF16),
            pltpu.VMEM(own, BF16),
            pltpu.VMEM(own, BF16),
            pltpu.VMEM(pairs, BF16),
            pltpu.VMEM(pairs, BF16),
            table,
            table,
            table,
            pltpu.VMEM((rows, 1), F32),
            pltpu.VMEM((rows, ff), F32),
            pltpu.VMEM((rows, ff), F32),
            wide,
            wide,
            wide,
            wide,
            pltpu.VMEM((mb, n, tok, width), F32),
            pltpu.VMEM((2,) + pairs, BF16),
            pltpu.VMEM((2,) + pairs, BF16),
            pltpu.VMEM((2,) + own, BF16),
            pltpu.VMEM((2,) + own, BF16),
            sem((3, mb, steps)),
            sem((3, mb, steps)),
            sem((3, mb, steps)),
            sem((3, mb, steps)),
            sem((2,)),
            sem((2,)),
            sem((8,)),
        ],
        compiler_params=pltpu.CompilerParams(
            collective_id=0, has_side_effects=True, vmem_limit_bytes=56 * 1024 * 1024
        ),
    )(
        inputs, route_ids[0], route_gates[0], cotangent, w_gate[0, 0], w_up[0, 0], w_down[0, 0]
    )
    section_out, grad_in, grad_gates, normed, scaled, grads, gate_pre, up_pre = outs
    normed = normed.reshape(rows, width)
    grads = grads.reshape(rows, width)

    def outer(a, b):
        return lax.dot_general(
            a, b, (((0,), (0,)), ((), ())), preferred_element_type=F32
        ).astype(BF16)[None, None]

    return (
        section_out[None],
        grad_in[None],
        grad_gates[None],
        outer(normed, gate_pre),
        outer(normed, up_pre),
        outer(scaled, grads),
    )


def solution(mesh):
    tokens = P(None, "expert", None)
    routed = P("section", None, "expert", None)
    held = P("section", "expert", None, None)
    return jax.shard_map(
        functools.partial(body, mesh.shape["section"], mesh.shape["expert"]),
        mesh=mesh,
        in_specs=(tokens, routed, routed, held, held, held, tokens),
        out_specs=(routed, routed, routed, held, held, held),
        check_vma=False,
    )
```

profile of v0, /device:TPU:0, one launch (start us, length us, event | category | flops | bytes accessed | tf_op | source)
XLA Modules:
  0.0 143.7 jit_solution(14583607433144843528)
XLA Ops:
  0.6 131.6 %shard_map.118 = (bf16[2,8,2048]{2,1,0:T(8,128)(2,1)}, bf16[2,8,2048]{2,1,0:T(8,128)(2,1)}, f32[2,8,8]{2,1,0:T(8,128)}, bf16[2,8,16,2048]{3,2,1,0:T(8,128)(2,1)}...) custom-call(bf16[2,8,2048]{2,1,0:T(8,128)(2,1)} %x_ref.1, ...), custom_call_target="tpu_custom_call" | custom-call | tf_op jit(solution)/shard_map/pallas_call | solution.py:349
  132.2 0.0 copy-start.4
  132.3 0.0 copy-start.6
  132.3 4.1 %fusion.1 = bf16[1,1,2048,768]{3,2,1,0:T(8,128)(2,1)} fusion(bf16[256,2048]{1,0:T(8,128)(2,1)} %bitcast.31, bf16[256,768]{1,0:T(8,128)(2,1)} %get-tuple-element.19), kind=kOutput, calls=%fused_computation.4 | convolution fusion | flops 806879232 | bytes 4587520 | tf_op jit(solution)/shard_map/dot_general | solution.py:408
  136.4 0.0 copy-done.4
  136.4 0.0 copy-done.6
  136.4 0.0 copy-start.3
  136.4 0.0 copy-start.5
  136.4 2.7 %fusion = bf16[1,1,2048,768]{3,2,1,0:T(8,128)(2,1)} fusion(bf16[256,2048]{1,0:T(8,128)(2,1)S(1)} %bitcast.32, bf16[256,768]{1,0:T(8,128)(2,1)S(1)} %copy-done.6), kind=kOutput, calls=%fused_computation.3 | convolution fusion | flops 806879232 | bytes 4587520 | tf_op jit(solution)/shard_map/dot_general | solution.py:408
  139.1 0.0 copy-done.3
  139.1 0.0 copy-done.5
  139.1 0.0 copy-start.1
  139.1 0.0 copy-start
  139.1 0.0 copy-start.2
  139.1 2.7 %fusion.2 = bf16[1,1,768,2048]{3,2,1,0:T(8,128)(2,1)} fusion(bf16[256,768]{1,0:T(8,128)(2,1)S(1)} %copy-done.5, bf16[256,2048]{1,0:T(8,128)(2,1)S(1)} %bitcast.30), kind=kOutput, calls=%fused_computation.5 | convolution fusion | flops 806879232 | bytes 4587520 | tf_op jit(solution)/shard_map/dot_general | solution.py:408
  141.8 0.0 copy-done.1
  141.8 0.6 copy.16
  142.4 0.0 copy-done
  142.4 0.6 copy.17
  143.1 0.0 copy-done.2
  143.1 0.6 copy.18
Async XLA Ops:
  132.2 4.1 %copy-start.4 = (bf16[2,8,16,2048]{3,2,1,0:T(8,128)(2,1)S(1)}, bf16[2,8,16,2048]{3,2,1,0:T(8,128)(2,1)}, u32[]{:S(2)}) copy-start(bf16[2,8,16,2048]{3,2,1,0:T(8,128)(2,1)} %get-tuple-element.17) | copy-start | bytes 3145732
  132.3 4.1 %copy-start.6 = (bf16[256,768]{1,0:T(8,128)(2,1)S(1)}, bf16[256,768]{1,0:T(8,128)(2,1)}, u32[]{:S(2)}) copy-start(bf16[256,768]{1,0:T(8,128)(2,1)} %get-tuple-element.18) | copy-start | bytes 1179652
  136.4 2.7 %copy-start.3 = (bf16[2,8,16,2048]{3,2,1,0:T(8,128)(2,1)S(1)}, bf16[2,8,16,2048]{3,2,1,0:T(8,128)(2,1)}, u32[]{:S(2)}) copy-start(bf16[2,8,16,2048]{3,2,1,0:T(8,128)(2,1)} %get-tuple-element.21) | copy-start | bytes 3145732
  136.4 2.7 %copy-start.5 = (bf16[256,768]{1,0:T(8,128)(2,1)S(1)}, bf16[256,768]{1,0:T(8,128)(2,1)}, u32[]{:S(2)}) copy-start(bf16[256,768]{1,0:T(8,128)(2,1)} %get-tuple-element.20) | copy-start | bytes 1179652
  139.1 2.7 %copy-start.1 = (bf16[2,8,2048]{2,1,0:T(8,128)(2,1)S(1)}, bf16[2,8,2048]{2,1,0:T(8,128)(2,1)}, u32[]{:S(2)}) copy-start(bf16[2,8,2048]{2,1,0:T(8,128)(2,1)} %get-tuple-element.14) | copy-start | bytes 196612
  139.1 3.3 %copy-start = (bf16[2,8,2048]{2,1,0:T(8,128)(2,1)S(1)}, bf16[2,8,2048]{2,1,0:T(8,128)(2,1)}, u32[]{:S(2)}) copy-start(bf16[2,8,2048]{2,1,0:T(8,128)(2,1)} %get-tuple-element.15) | copy-start | bytes 196612
  139.1 4.0 %copy-start.2 = (f32[2,8,8]{2,1,0:T(8,128)S(1)}, f32[2,8,8]{2,1,0:T(8,128)}, u32[]{:S(2)}) copy-start(f32[2,8,8]{2,1,0:T(8,128)} %get-tuple-element.16) | copy-start | bytes 1540
where the time goes:
time: 144 us
  Pallas kernels  132 us (92%)
  matrix products  9.5 us (7%)
  local copies, waits for them, and re-layouts  1.89 us (1%)
    pallas_call x1, Pallas kernels, body(): pl.pallas_call(functools.partial(kernel, sections, n), out_shape=(jax.Sha...  132 us
    dot_general x3, matrix products, outer(): lax.dot_general(a, b, (((0,), (0,)), ((), ())), preferred_element_type=F32)  9.5 us

commit v1 on v0

--- a/solution.py
+++ b/solution.py
@@ -12,17 +12,22 @@
 BF16 = jnp.bfloat16
 LANES = 128
 TILE = 256
+STAGED = 4
 
 
 def nt_dot(a, b):
     return lax.dot_general(a, b, (((1,), (1,)), ((), ())), preferred_element_type=F32)
 
 
-def bit_orders(n):
+def bit_groups(n):
     bits = n.bit_length() - 1
-    high_first = list(range(bits - 1, -1, -1))
-    across = [1] + [b for b in high_first if b not in (0, 1)] + [0]
-    return high_first, across
+    far = list(range(bits - 1, 1, -1))
+    far = [tuple(far[i : i + 2]) for i in range(0, len(far), 2)]
+    return far + [(1,), (0,)], [(1,)] + far + [(0,)]
+
+
+def flip_mask(group, d):
+    return sum(1 << b for i, b in enumerate(group) if (d >> i) & 1)
 
 
 def kernel(
@@ -41,27 +46,44 @@
     me = lax.axis_index("expert")
     sec = lax.axis_index("section")
     last = sections - 1
-    orders = [bit_orders(n)[m % 2] for m in range(mb)]
+    groups = [bit_groups(n)[m % 2] for m in range(mb)]
 
     def bit_of(b):
         return (me // (1 << b)) % 2
 
-    def peer(b):
-        return me + (1 << b) * (1 - 2 * bit_of(b))
-
-    place = [sum(bit_of(b) * (1 << k) for k, b in enumerate(order)) for order in orders]
-
-    def other(m, k):
+    def flipped(mask):
+        return me + sum(
+            (1 << b) * (1 - 2 * bit_of(b)) for b in range(steps) if (mask >> b) & 1
+        )
+
+    stages, place = [], []
+    for group in groups:
+        listed, at, r = [], 0, 0
+        for bits in group:
+            listed.append((at, bits))
+            r = r + sum(bit_of(b) * (1 << (at + i)) for i, b in enumerate(bits))
+            at += len(bits)
+        stages.append(listed)
+        place.append(r)
+    depth = len(stages[0])
+
+    def other(m, low, d):
         r = place[m]
-        return r + (1 << k) * (1 - 2 * ((r // (1 << k)) % 2))
-
-    def base_of(r, k):
-        return (r // (1 << k)) * (1 << k)
-
-    def remote(src, dst, ssem, rsem, b):
+        for i in range(steps):
+            if ((d << low) >> i) & 1:
+                r = r + (1 << i) * (1 - 2 * ((place[m] // (1 << i)) % 2))
+        return r
+
+    def diffs(m, s):
+        return range(1, 1 << len(stages[m][s][1]))
+
+    def base_of(r, low):
+        return (r // (1 << low)) * (1 << low)
+
+    def remote(src, dst, ssem, rsem, mask):
         return pltpu.make_async_remote_copy(
             src_ref=src, dst_ref=dst, send_sem=ssem, recv_sem=rsem,
-            device_id={"expert": peer(b)}, device_id_type=pl.DeviceIdType.MESH,
+            device_id={"expert": flipped(mask)}, device_id_type=pl.DeviceIdType.MESH,
         )
 
     weights = [
@@ -72,9 +94,13 @@
         c.start()
 
     barrier = pltpu.get_barrier_semaphore()
-    for b in range(steps):
+    masks = sorted(
+        {flip_mask(bits, d) for group in groups for bits in group for d in range(1, 1 << len(bits))}
+    )
+    for mask in masks:
         pl.semaphore_signal(
-            barrier, inc=1, device_id={"expert": peer(b)}, device_id_type=pl.DeviceIdType.MESH
+            barrier, inc=1, device_id={"expert": flipped(mask)},
+            device_id_type=pl.DeviceIdType.MESH,
         )
 
     def hello(ok, step):
@@ -98,40 +124,72 @@
         tg[m, place[m]] = dense
 
     beside = (sec > 0).astype(jnp.int32) + (sec < last).astype(jnp.int32)
-    pl.semaphore_wait(barrier, steps + beside)
-
-    def small_copy(m, k):
-        part = tg.at[m, pl.ds(base_of(place[m], k), 1 << k)]
-        return remote(part, part, ag_s.at[0, m, k], ag_r.at[0, m, k], orders[m][k])
-
-    def row_copy(which, own, staged, full, m, k):
-        sems = ag_s.at[which, m, k], ag_r.at[which, m, k]
-        if k == 0:
-            return remote(own.at[m], staged.at[m], *sems, orders[m][0])
-        part = full.at[m, pl.ds(base_of(place[m], k) // 2, 1 << (k - 1))]
-        return remote(part, part, *sems, orders[m][k])
-
-    def gather_rows(which, own, staged, full):
-        for k in range(steps):
-            copies = [row_copy(which, own, staged, full, m, k) for m in range(mb)]
-            for c in copies:
-                c.start()
-            for m, c in enumerate(copies):
-                c.wait()
-                if k == 0:
-                    mine = own[m].astype(F32)
-                    theirs = staged[m].astype(F32)
-                    low = place[m] % 2 == 0
-                    pair = jnp.concatenate(
-                        [jnp.where(low, mine, theirs), jnp.where(low, theirs, mine)], axis=0
-                    )
-                    full[m, place[m] // 2] = pair.astype(BF16)
-
-    def table_copy(m, k):
-        theirs = base_of(other(m, k), k)
+    pl.semaphore_wait(barrier, len(masks) + beside)
+
+    def small_copy(m, s, d):
+        low, bits = stages[m][s]
+        part = tg.at[m, pl.ds(base_of(place[m], low), 1 << low)]
         return remote(
-            tt.at[m, pl.ds(theirs, 1 << k)], ttr.at[m, pl.ds(1 << k, 1 << k)],
-            rs_s.at[2, m, k], rs_r.at[2, m, k], orders[m][k],
+            part, part, ag_s.at[0, m, d << low], ag_r.at[0, m, d << low], flip_mask(bits, d)
+        )
+
+    def row_copy(which, own, staged, full, m, s, d):
+        low, bits = stages[m][s]
+        sems = ag_s.at[which, m, d << low], ag_r.at[which, m, d << low]
+        if low == 0:
+            return remote(own.at[m], staged.at[m, d], *sems, flip_mask(bits, d))
+        part = full.at[m, pl.ds(base_of(place[m], low) // 2, 1 << (low - 1))]
+        return remote(part, part, *sems, flip_mask(bits, d))
+
+    def every(build, act):
+        for s in range(depth):
+            for m in range(mb):
+                for d in diffs(m, s):
+                    act(build(m, s, d))
+
+    def gather_rows(rows_of, small):
+        for s in range(depth):
+            for m in range(mb):
+                for d in diffs(m, s):
+                    if rows_of is not None:
+                        row_copy(*rows_of, m, s, d).start()
+                    if small:
+                        small_copy(m, s, d).start()
+            for m in range(mb):
+                for d in diffs(m, s):
+                    if rows_of is not None:
+                        row_copy(*rows_of, m, s, d).wait_recv()
+                    if small:
+                        small_copy(m, s, d).wait_recv()
+                if s == 0 and rows_of is not None:
+                    _, own, staged, full = rows_of
+                    even = place[m] % 2 == 0
+                    for p in range(1 << (len(stages[m][0][1]) - 1)):
+                        near = own[m] if p == 0 else staged[m, 2 * p]
+                        near, off = near.astype(F32), staged[m, 2 * p + 1].astype(F32)
+                        pair = jnp.concatenate(
+                            [jnp.where(even, near, off), jnp.where(even, off, near)], axis=0
+                        )
+                        full[m, other(m, 0, 2 * p) // 2] = pair.astype(BF16)
+
+    def table_copy(m, s, d):
+        low, bits = stages[m][s]
+        theirs = base_of(other(m, low, d), low)
+        return remote(
+            tt.at[m, pl.ds(theirs, 1 << low)], ttr.at[m, pl.ds(d << low, 1 << low)],
+            rs_s.at[2, m, d << low], rs_r.at[2, m, d << low], flip_mask(bits, d),
+        )
+
+    def sum_copy(which, m, s, d):
+        low, bits = stages[m][s]
+        sems = rs_s.at[which, m, d << low], rs_r.at[which, m, d << low]
+        if low == 0:
+            return remote(sb0.at[which, m, d], rb0.at[which, m, d], *sems, flip_mask(bits, d))
+        half = 1 << (low - 1)
+        theirs = base_of(other(m, low, d), low)
+        return remote(
+            sb.at[which, m, pl.ds(theirs // 2, half)], rb.at[which, m, pl.ds(d * half, half)],
+            *sems, flip_mask(bits, d),
         )
 
     def reduce_rows(which, table):
@@ -141,94 +199,105 @@
             elif table is not None:
                 pl.when(table)(act)
 
-        def row_part(m, k):
-            sems = rs_s.at[which, m, k], rs_r.at[which, m, k]
-            theirs = base_of(other(m, k), k)
-            if k == 0:
-                sb0[which, m] = acc[m, theirs].astype(BF16)
-                return remote(sb0.at[which, m], rb0.at[which, m], *sems, orders[m][0])
-            half = 1 << (k - 1)
-
-            def pack(i, carry):
+        def pack(m, low, d):
+            theirs = base_of(other(m, low, d), low)
+            if low == 0:
+                sb0[which, m, d] = acc[m, theirs].astype(BF16)
+                return
+
+            def one(i, carry):
                 pair = acc[m, pl.ds(theirs + 2 * i, 2)].reshape(2 * tok, width)
                 sb[which, m, theirs // 2 + i] = pair.astype(BF16)
                 return carry
 
-            lax.fori_loop(0, half, pack, 0)
-            return remote(
-                sb.at[which, m, pl.ds(theirs // 2, half)], rb.at[which, m, pl.ds(half, half)],
-                *sems, orders[m][k],
-            )
-
-        for k in reversed(range(steps)):
-            copies = []
+            lax.fori_loop(0, 1 << (low - 1), one, 0)
+
+        for s in reversed(range(depth)):
             for m in range(mb):
-                copies.append(row_part(m, k))
-                copies[m].start()
+                for d in diffs(m, s):
+                    pack(m, stages[m][s][0], d)
+                    sum_copy(which, m, s, d).start()
 
             def start_tables():
                 for m in range(mb):
-                    table_copy(m, k).start()
+                    for d in diffs(m, s):
+                        table_copy(m, s, d).start()
 
             when_table(start_tables)
             for m in range(mb):
-                copies[m].wait()
-                mine = base_of(place[m], k)
-                if k == 0:
-                    acc[m, mine] = acc[m, mine] + rb0[which, m].astype(F32)
+                low = stages[m][s][0]
+                mine = base_of(place[m], low)
+                for d in diffs(m, s):
+                    sum_copy(which, m, s, d).wait_recv()
+                if low == 0:
+                    whole = acc[m, mine]
+                    for d in diffs(m, s):
+                        whole = whole + rb0[which, m, d].astype(F32)
+                    acc[m, mine] = whole
                 else:
-                    half = 1 << (k - 1)
+                    half = 1 << (low - 1)
 
                     def add(i, carry):
-                        got = rb[which, m, half + i].astype(F32).reshape(2, tok, width)
                         spot = pl.ds(mine + 2 * i, 2)
-                        acc[m, spot] = acc[m, spot] + got
+                        whole = acc[m, spot]
+                        for d in diffs(m, s):
+                            got = rb[which, m, d * half + i].astype(F32)
+                            whole = whole + got.reshape(2, tok, width)
+                        acc[m, spot] = whole
                         return carry
 
                     lax.fori_loop(0, half, add, 0)
 
             def finish_tables():
                 for m in range(mb):
-                    table_copy(m, k).wait()
-                    mine = pl.ds(base_of(place[m], k), 1 << k)
-                    tt[m, mine] = tt[m, mine] + ttr[m, pl.ds(1 << k, 1 << k)]
+                    low = stages[m][s][0]
+                    mine = pl.ds(base_of(place[m], low), 1 << low)
+                    for d in diffs(m, s):
+                        table_copy(m, s, d).wait_recv()
+                        tt[m, mine] = tt[m, mine] + ttr[m, pl.ds(d << low, 1 << low)]
 
             when_table(finish_tables)
 
+    x_rows = (1, nown, xst, agx)
+    g_rows = (2, gin, gst, agg)
+
+    def normalize():
+        x_float = xin[...].astype(F32)
+        scale = lax.rsqrt(jnp.mean(x_float * x_float, axis=-1, keepdims=True) + EPS)
+        nown[...] = (x_float * scale).astype(BF16)
+
+    def relay(which, src, dst, step):
+        return pltpu.make_async_remote_copy(
+            src_ref=src, dst_ref=dst, send_sem=rl_s.at[which], recv_sem=rl_r.at[which],
+            device_id={"section": sec + step}, device_id_type=pl.DeviceIdType.MESH,
+        )
+
     @pl.when(sec == last)
     def _():
         gin[...] = cot_ref[...]
-        gather_rows(2, gin, gst, agg)
-
-    for k in range(steps):
-        copies = [small_copy(m, k) for m in range(mb)]
-        for c in copies:
-            c.start()
-        for c in copies:
-            c.wait()
+        gather_rows(g_rows, True)
+
+    @pl.when(sec == 0)
+    def _():
+        xin[...] = x_ref[...]
+        normalize()
+        gather_rows(x_rows, last > 0)
+
+    @pl.when((sec > 0) & (sec < last))
+    def _():
+        gather_rows(None, True)
+
+    @pl.when(sec > 0)
+    def _():
+        relay(0, so_ref, xin, 0).wait_recv()
+        normalize()
+        gather_rows(x_rows, False)
+
     all_lanes = lax.broadcasted_iota(jnp.int32, (rows, LANES), 1)
     gc[...] = jnp.sum(
         jnp.where(all_lanes == me, tg[...].reshape(rows, LANES), 0.0), axis=1, keepdims=True
     )
 
-    def relay(which, src, dst, step):
-        return pltpu.make_async_remote_copy(
-            src_ref=src, dst_ref=dst, send_sem=rl_s.at[which], recv_sem=rl_r.at[which],
-            device_id={"section": sec + step}, device_id_type=pl.DeviceIdType.MESH,
-        )
-
-    @pl.when(sec == 0)
-    def _():
-        xin[...] = x_ref[...]
-
-    @pl.when(sec > 0)
-    def _():
-        relay(0, so_ref, xin, 0).wait_recv()
-
-    x_float = xin[...].astype(F32)
-    scale = lax.rsqrt(jnp.mean(x_float * x_float, axis=-1, keepdims=True) + EPS)
-    nown[...] = (x_float * scale).astype(BF16)
-    gather_rows(1, nown, xst, agx)
     keep = [pltpu.make_async_copy(agx, nx_hbm, loc.at[3])]
     keep[0].start()
     for c in weights:
@@ -263,7 +332,7 @@
         down_and_out(None)
         relay(0, so_ref, xin, 1).start()
         relay(1, gi_ref, gin, 0).wait_recv()
-        gather_rows(2, gin, gst, agg)
+        gather_rows(g_rows, False)
 
     keep.append(pltpu.make_async_copy(agg, ag_hbm, loc.at[4]))
     keep[1].start()
@@ -329,6 +398,12 @@
     def _():
         relay(1, gi_ref, gin, -1).wait_send()
 
+    every(small_copy, lambda c: c.wait_send())
+    every(table_copy, lambda c: c.wait_send())
+    for rows_of in (x_rows, g_rows):
+        every(functools.partial(row_copy, *rows_of), lambda c: c.wait_send())
+    for which in range(2):
+        every(functools.partial(sum_copy, which), lambda c: c.wait_send())
     for c in keep:
         c.wait()
 
@@ -338,9 +413,9 @@
     top = route_ids.shape[3]
     ff = w_gate.shape[3]
     rows = mb * n * tok
-    steps = n.bit_length() - 1
     pairs = (mb, n // 2, 2 * tok, width)
     own = (mb, tok, width)
+    staged = (mb, STAGED, tok, width)
     vmem = pl.BlockSpec(memory_space=pltpu.VMEM)
     anywhere = pl.BlockSpec(memory_space=pl.ANY)
     sem = pltpu.SemaphoreType.DMA
@@ -367,8 +442,8 @@
             pltpu.VMEM(own, BF16),
             pltpu.VMEM(own, BF16),
             pltpu.VMEM(own, BF16),
-            pltpu.VMEM(own, BF16),
-            pltpu.VMEM(own, BF16),
+            pltpu.VMEM(staged, BF16),
+            pltpu.VMEM(staged, BF16),
             pltpu.VMEM(pairs, BF16),
             pltpu.VMEM(pairs, BF16),
             table,
@@ -384,12 +459,12 @@
             pltpu.VMEM((mb, n, tok, width), F32),
             pltpu.VMEM((2,) + pairs, BF16),
             pltpu.VMEM((2,) + pairs, BF16),
-            pltpu.VMEM((2,) + own, BF16),
-            pltpu.VMEM((2,) + own, BF16),
-            sem((3, mb, steps)),
-            sem((3, mb, steps)),
-            sem((3, mb, steps)),
-            sem((3, mb, steps)),
+            pltpu.VMEM((2,) + staged, BF16),
+            pltpu.VMEM((2,) + staged, BF16),
+            sem((3, mb, n)),
+            sem((3, mb, n)),
+            sem((3, mb, n)),
+            sem((3, mb, n)),
             sem((2,)),
             sem((2,)),
             sem((8,)),

time: 144 us -> 123 us (0.85)
  Pallas kernels: 132 us -> 110 us
    pallas_call x1, Pallas kernels: 132 us -> 110 us  [body(): pl.pallas_call(functools.partial(kernel, sections, n), out_shape=(jax.Sha...]
where the time goes in v1:
time: 123 us; the launch traced here: 122 us
  Pallas kernels  110 us (89%)
  matrix products  9.5 us (8%)
  local copies, waits for them, and re-layouts  1.89 us (2%)
    pallas_call x1, Pallas kernels, body(): pl.pallas_call(functools.partial(kernel, sections, n), out_shape=(jax.Sha...  110 us
    dot_general x3, matrix products, outer(): lax.dot_general(a, b, (((0,), (0,)), ((), ())), preferred_element_type=F32)  9.5 us

profile of v1, /device:TPU:0, one launch (start us, length us, event | category | flops | bytes accessed | tf_op | source)
XLA Modules:
  0.0 122.3 jit_solution(2904794444511494246)
XLA Ops:
  0.6 110.3 %shard_map.118 = (bf16[2,8,2048]{2,1,0:T(8,128)(2,1)}, bf16[2,8,2048]{2,1,0:T(8,128)(2,1)}, f32[2,8,8]{2,1,0:T(8,128)}, bf16[2,8,16,2048]{3,2,1,0:T(8,128)(2,1)}...) custom-call(bf16[2,8,2048]{2,1,0:T(8,128)(2,1)} %x_ref.1, ...), custom_call_target="tpu_custom_call" | custom-call | tf_op jit(solution)/shard_map/pallas_call | solution.py:424
  110.9 0.0 copy-start.4
  110.9 0.0 copy-start.6
  110.9 4.1 %fusion.1 = bf16[1,1,2048,768]{3,2,1,0:T(8,128)(2,1)} fusion(bf16[256,2048]{1,0:T(8,128)(2,1)} %bitcast.31, bf16[256,768]{1,0:T(8,128)(2,1)} %get-tuple-element.19), kind=kOutput, calls=%fused_computation.4 | convolution fusion | flops 806879232 | bytes 4587520 | tf_op jit(solution)/shard_map/dot_general | solution.py:483
  115.0 0.0 copy-done.4
  115.1 0.0 copy-done.6
  115.1 0.0 copy-start.3
  115.1 0.0 copy-start.5
  115.1 2.7 %fusion = bf16[1,1,2048,768]{3,2,1,0:T(8,128)(2,1)} fusion(bf16[256,2048]{1,0:T(8,128)(2,1)S(1)} %bitcast.32, bf16[256,768]{1,0:T(8,128)(2,1)S(1)} %copy-done.6), kind=kOutput, calls=%fused_computation.3 | convolution fusion | flops 806879232 | bytes 4587520 | tf_op jit(solution)/shard_map/dot_general | solution.py:483
  117.8 0.0 copy-done.3
  117.8 0.0 copy-done.5
  117.8 0.0 copy-start.1
  117.8 0.0 copy-start
  117.8 0.0 copy-start.2
  117.8 2.7 %fusion.2 = bf16[1,1,768,2048]{3,2,1,0:T(8,128)(2,1)} fusion(bf16[256,768]{1,0:T(8,128)(2,1)S(1)} %copy-done.5, bf16[256,2048]{1,0:T(8,128)(2,1)S(1)} %bitcast.30), kind=kOutput, calls=%fused_computation.5 | convolution fusion | flops 806879232 | bytes 4587520 | tf_op jit(solution)/shard_map/dot_general | solution.py:483
  120.5 0.0 copy-done.1
  120.5 0.6 copy.16
  121.1 0.0 copy-done
  121.1 0.6 copy.17
  121.7 0.0 copy-done.2
  121.7 0.6 copy.18
Async XLA Ops:
  110.9 4.1 %copy-start.4 = (bf16[2,8,16,2048]{3,2,1,0:T(8,128)(2,1)S(1)}, bf16[2,8,16,2048]{3,2,1,0:T(8,128)(2,1)}, u32[]{:S(2)}) copy-start(bf16[2,8,16,2048]{3,2,1,0:T(8,128)(2,1)} %get-tuple-element.17) | copy-start | bytes 3145732
  110.9 4.1 %copy-start.6 = (bf16[256,768]{1,0:T(8,128)(2,1)S(1)}, bf16[256,768]{1,0:T(8,128)(2,1)}, u32[]{:S(2)}) copy-start(bf16[256,768]{1,0:T(8,128)(2,1)} %get-tuple-element.18) | copy-start | bytes 1179652
  115.1 2.7 %copy-start.3 = (bf16[2,8,16,2048]{3,2,1,0:T(8,128)(2,1)S(1)}, bf16[2,8,16,2048]{3,2,1,0:T(8,128)(2,1)}, u32[]{:S(2)}) copy-start(bf16[2,8,16,2048]{3,2,1,0:T(8,128)(2,1)} %get-tuple-element.21) | copy-start | bytes 3145732
  115.1 2.7 %copy-start.5 = (bf16[256,768]{1,0:T(8,128)(2,1)S(1)}, bf16[256,768]{1,0:T(8,128)(2,1)}, u32[]{:S(2)}) copy-start(bf16[256,768]{1,0:T(8,128)(2,1)} %get-tuple-element.20) | copy-start | bytes 1179652
  117.8 2.7 %copy-start.1 = (bf16[2,8,2048]{2,1,0:T(8,128)(2,1)S(1)}, bf16[2,8,2048]{2,1,0:T(8,128)(2,1)}, u32[]{:S(2)}) copy-start(bf16[2,8,2048]{2,1,0:T(8,128)(2,1)} %get-tuple-element.14) | copy-start | bytes 196612
  117.8 3.3 %copy-start = (bf16[2,8,2048]{2,1,0:T(8,128)(2,1)S(1)}, bf16[2,8,2048]{2,1,0:T(8,128)(2,1)}, u32[]{:S(2)}) copy-start(bf16[2,8,2048]{2,1,0:T(8,128)(2,1)} %get-tuple-element.15) | copy-start | bytes 196612
  117.8 4.0 %copy-start.2 = (f32[2,8,8]{2,1,0:T(8,128)S(1)}, f32[2,8,8]{2,1,0:T(8,128)}, u32[]{:S(2)}) copy-start(f32[2,8,8]{2,1,0:T(8,128)} %get-tuple-element.16) | copy-start | bytes 1540
